TPU v7x, 256 devices: a whole 4x4x8 slice. The times are simulated.
256 devices in a mesh: row: 32 (over z, x), col: 4 (over y), depth: 2 (over core).
Axes of the slice: x: 4, y: 4, z: 8, core: 2. Of those that a mesh axis runs over, the one named last changes fastest.
Arguments:
- layer_input: bfloat16 [3072, 4096], P(('depth', 'col'), 'row'), may hold values from -1.796875 to 1.796875
- gate_pre: bfloat16 [3072, 14784], P(('depth', 'row'), 'col'), may hold values from -9 to 9
- up_pre: bfloat16 [3072, 14784], P(('depth', 'row'), 'col'), may hold values from -6 to 6
- hidden_grad: bfloat16 [3072, 14784], P(('depth', 'row'), 'col'), may hold values from -2.5 to 2.5
- gate_weight: bfloat16 [4096, 14784], P('row', 'col'), may hold values from -0.09375 to 0.09375
- up_weight: bfloat16 [4096, 14784], P('row', 'col'), may hold values from -0.09375 to 0.09375
Outputs:
- input_grad: bfloat16 [3072, 4096], P(('depth', 'col'), 'row')
- gate_weight_grad: bfloat16 [4096, 14784], P(('row', 'depth'), 'col')
- up_weight_grad: bfloat16 [4096, 14784], P(('row', 'depth'), 'col')
All inputs are finite; a program needn't handle non-finite values.
Results may differ from a plain program's by a relative error of at most 0.014.
Values may be sent and summed in bfloat16 or wider, within the bound.
A program may use at most 128 MiB of HBM per device.

v0:
```python
import jax
import jax.numpy as jnp
from jax import lax
from jax.sharding import PartitionSpec as P


def swiglu_back(gate_pre, up_pre, hidden_grad):
    gate_f = gate_pre.astype(jnp.float32)
    up_f = up_pre.astype(jnp.float32)
    grad_f = hidden_grad.astype(jnp.float32)
    sigma = jax.nn.sigmoid(gate_f)
    gate_grad = (grad_f * up_f * sigma * (1.0 + gate_f * (1.0 - sigma))).astype(jnp.bfloat16)
    up_grad = (grad_f * gate_f * sigma).astype(jnp.bfloat16)
    return (gate_grad, up_grad)


def on_device(layer_input, gate_pre, up_pre, hidden_grad, gate_weight, up_weight):
    layer_x = lax.all_gather(layer_input, "col", axis=0, tiled=True)
    gate_all, up_all, grad_all = (
        lax.all_gather(gate_pre, "row", axis=0, tiled=True),
        lax.all_gather(up_pre, "row", axis=0, tiled=True),
        lax.all_gather(hidden_grad, "row", axis=0, tiled=True),
    )
    gate_grad, up_grad = swiglu_back(gate_all, up_all, grad_all)
    term = lax.dot_general(
        gate_grad, gate_weight, (((1,), (1,)), ((), ())), preferred_element_type=jnp.float32
    )
    input_grad = lax.psum_scatter(
        (
            term
            + lax.dot_general(
                up_grad, up_weight, (((1,), (1,)), ((), ())), preferred_element_type=jnp.float32
            )
        ).astype(jnp.bfloat16),
        "col",
        scatter_dimension=0,
        tiled=True,
    )
    half_cols = gate_weight.shape[1]
    gate_part = lax.dot_general(
        layer_x, gate_grad, (((0,), (0,)), ((), ())), preferred_element_type=jnp.float32
    )
    up_part = lax.dot_general(
        layer_x, up_grad, (((0,), (0,)), ((), ())), preferred_element_type=jnp.float32
    )
    summed = lax.psum_scatter(
        jnp.concatenate([gate_part, up_part], axis=1).astype(jnp.bfloat16),
        "depth",
        scatter_dimension=0,
        tiled=True,
    ).astype(jnp.float32)
    return (
        input_grad,
        summed[:, :half_cols].astype(jnp.bfloat16),
        summed[:, half_cols:].astype(jnp.bfloat16),
    )


def solution(mesh):
    placed = (
        P(("depth", "col"), "row"),
        P(("depth", "row"), "col"),
        P(("depth", "row"), "col"),
        P(("depth", "row"), "col"),
        P("row", "col"),
        P("row", "col"),
    )
    return jax.shard_map(
        on_device,
        mesh=mesh,
        in_specs=placed,
        out_specs=(
            P(("depth", "col"), "row"),
            P(("row", "depth"), "col"),
            P(("row", "depth"), "col"),
        ),
        check_vma=False,
    )
```

profile of v0, /device:TPU:16, one launch (start us, length us, event | category | flops | bytes accessed | tf_op | source)
XLA Modules:
  0.0 425.2 jit_solution(10710579339562138863)
XLA Ops:
  7.2 0.0 all-gather.8.cloned.1.call-start
  7.2 0.7 all-gather.8.cloned.1.call-update
  7.9 0.0 all-gather.6.cloned.1.call-start
  8.0 0.7 all-gather.6.cloned.1.call-update
  8.7 0.0 all-gather.4.cloned.1.call-start
  8.7 0.7 all-gather.4.cloned.1.call-update
  9.4 0.0 reduce-scatter.7.cloned.1.call-start
  9.4 13.2 %all_gather.15 = bf16[1536,128]{1,0:T(8,128)(2,1)S(1)} all-gather(bf16[384,128]{1,0:T(8,128)(2,1)} %param.6), channel_id=1, replica_groups=mesh['row'=32,'col'=4,'depth'=2] {'col'}, dimensions={0}, use_global_device_ids=true | all-gather | bytes 491520 | tf_op jit(solution)/shard_map/all_gather | solution.py:18
  22.6 104.5 %all-gather.8.cloned.1.call-done = bf16[1536,3696]{1,0:T(8,128)(2,1)} async-done(((bf16[48,3696]{1,0:T(8,128)(2,1)}), bf16[1536,3696]{1,0:T(8,128)(2,1)}) %all-gather.8.cloned.1.call-update) | async-done | bytes 11354128 | tf_op jit(solution)/shard_map/all_gather | solution.py:20
  127.1 113.4 %all-gather.6.cloned.1.call-done = bf16[1536,3696]{1,0:T(8,128)(2,1)} async-done(((bf16[48,3696]{1,0:T(8,128)(2,1)}), bf16[1536,3696]{1,0:T(8,128)(2,1)}) %all-gather.6.cloned.1.call-update) | async-done | bytes 11354128 | tf_op jit(solution)/shard_map/all_gather | solution.py:21
  240.6 113.4 %all-gather.4.cloned.1.call-done = bf16[1536,3696]{1,0:T(8,128)(2,1)} async-done(((bf16[48,3696]{1,0:T(8,128)(2,1)}), bf16[1536,3696]{1,0:T(8,128)(2,1)}) %all-gather.4.cloned.1.call-update) | async-done | bytes 11354128 | tf_op jit(solution)/shard_map/all_gather | solution.py:22
  354.0 16.1 %fusion.8 = (bf16[1536,3696]{1,0:T(8,128)(2,1)S(1)}, bf16[1536,3696]{1,0:T(8,128)(2,1)S(1)}) fusion(bf16[1536,3696]{1,0:T(8,128)(2,1)} %all-gather.8.cloned.1.call-done, bf16[1536,3696]{1,0:T(8,128)(2,1)} %all-gather.4.cloned.1.call-done, bf16[1536,3696]{1,0:T(8,128)(2,1)} %all-gather.6.cloned.1.call-done), kind=kLoop, calls=%fused_computation.12 | loop fusion | flops 90832896 | bytes 56770560 | tf_op jit(solution)/shard_map/convert_element_type | solution.py:13
  370.2 3.3 fusion.9
  373.4 3.3 fusion.10
  376.7 1.0 copy-done.3
  377.7 0.1 pad_maximum_fusion
  377.8 2.5 copy.13
  380.3 0.2 reduce-scatter.5.cloned.1.call-start
  380.6 6.1 %fusion.13 = f32[1536,128]{1,0:T(8,128)S(1)} fusion(bf16[1536,3696]{1,0:T(8,128)(2,1)} %copy-done.3, bf16[128,3696]{0,1:T(8,128)(2,1)S(1)} %copy-done), kind=kOutput, calls=%fused_computation.21 | convolution fusion | flops 1453326336 | bytes 13086720 | tf_op jit(solution)/shard_map/dot_general | solution.py:25
  386.7 1.5 copy-done.2
  388.2 4.0 fusion.11
  392.2 0.1 reduce-scatter.7.cloned.1.call-done
  392.3 2.3 fusion.12
  394.6 24.1 %reduce-scatter.5.cloned.1.call-done = bf16[384,128]{1,0:T(8,128)(2,1)} async-done(((bf16[1536,128]{1,0:T(8,128)(2,1)}), bf16[384,128]{1,0:T(8,128)(2,1)}) %reduce-scatter.5.cloned.1.call-update) | async-done | bytes 98320 | tf_op jit(solution)/shard_map/reduce_scatter | solution.py:28
  (10 shorter events, 0.1 us)
Async XLA Ops:
  7.2 373.4 %copy-start = (bf16[128,3696]{0,1:T(8,128)(2,1)S(1)}, bf16[128,3696]{0,1:T(8,128)(2,1)}, u32[]{:S(2)}) copy-start(bf16[128,3696]{0,1:T(8,128)(2,1)} %param.10) | copy-start | bytes 2838532
  7.2 120.0 %all-gather.8.cloned.1.call-start = ((), (), s32[]{:S(2)}) async-start(), calls=%async_computation.4 | async-start | bytes 11759616 | tf_op jit(solution)/shard_map/all_gather | solution.py:20
  7.9 232.7 %all-gather.6.cloned.1.call-start = ((), (), s32[]{:S(2)}) async-start(), calls=%async_computation.3 | async-start | bytes 11759616 | tf_op jit(solution)/shard_map/all_gather | solution.py:21
  8.7 345.3 %all-gather.4.cloned.1.call-start = ((), (), s32[]{:S(2)}) async-start(), calls=%async_computation.2 | async-start | bytes 11759616 | tf_op jit(solution)/shard_map/all_gather | solution.py:22
  9.4 383.0 %reduce-scatter.7.cloned.1.call-start = ((), (), s32[]{:S(2)}) async-start(), calls=%async_computation.6 | async-start | bytes 2850816
  370.1 6.6 %copy-start.1 = (bf16[1536,3696]{1,0:T(8,128)(2,1)}, bf16[1536,3696]{1,0:T(8,128)(2,1)S(1)}, u32[]{:S(2)}) copy-start(bf16[1536,3696]{1,0:T(8,128)(2,1)S(1)} %get-tuple-element.9) | copy-start | bytes 34062340
  370.1 7.6 %copy-start.3 = (bf16[1536,3696]{1,0:T(8,128)(2,1)}, bf16[1536,3696]{1,0:T(8,128)(2,1)S(1)}, u32[]{:S(2)}) copy-start(bf16[1536,3696]{1,0:T(8,128)(2,1)S(1)} %get-tuple-element.10) | copy-start | bytes 34062340
  380.3 6.4 %copy-start.4 = (bf16[128,3696]{0,1:T(8,128)(2,1)S(1)}, bf16[128,3696]{0,1:T(8,128)(2,1)}, u32[]{:S(2)}) copy-start(bf16[128,3696]{0,1:T(8,128)(2,1)} %param.11) | copy-start | bytes 2838532
  380.3 38.3 %reduce-scatter.5.cloned.1.call-start = ((), (), s32[]{:S(2)}) async-start(), calls=%async_computation.5 | async-start | bytes 491520 | tf_op jit(solution)/shard_map/reduce_scatter | solution.py:28
  380.6 7.6 %copy-start.2 = (bf16[1536,3696]{1,0:T(8,128)(2,1)S(1)}, bf16[1536,3696]{1,0:T(8,128)(2,1)}, u32[]{:S(2)}) copy-start(bf16[1536,3696]{1,0:T(8,128)(2,1)} %copy-done.1) | copy-start | bytes 34062340
Sparse Core Ops, SparseCore 0:
  10.6 116.4 all-gather.7
  129.7 110.7 all-gather.5
  243.2 110.7 all-gather.3
  380.5 11.8 reduce-scatter.6
  395.5 23.1 reduce-scatter.4
where the time goes:
time: 427 us; the launch traced here: 425 us
  waiting for transfers between devices  358 us (84%)
  matrix products  16.6 us (4%)
  other arithmetic  16.2 us (4%)
  between operations  13.9 us (3%)
  blocking collectives  13.2 us (3%)
  local copies, waits for them, and re-layouts  7.23 us (2%)
    all_gather x1, waiting for transfers between devices, on_device(): lax.all_gather(hidden_grad, 'row', axis=0, tiled=True)  113 us
    all_gather x1, waiting for transfers between devices, on_device(): lax.all_gather(up_pre, 'row', axis=0, tiled=True)  113 us
    all_gather x1, waiting for transfers between devices, on_device(): lax.all_gather(gate_pre, 'row', axis=0, tiled=True)  104 us
    reduce_scatter x1, waiting for transfers between devices, on_device(): lax.psum_scatter((term + lax.dot_general(up_grad, up_weight, (((1,), (1,)...  24.1 us
    convert_element_type x1, other arithmetic, swiglu_back(): up_grad = (grad_f * gate_f * sigma).astype(jnp.bfloat16)  16.1 us
    all_gather x1, blocking collectives, on_device(): layer_x = lax.all_gather(layer_input, 'col', axis=0, tiled=True)  13.2 us
  transfers between devices with their start and end apart: 5, of which 5 were waited for; matrix products, arithmetic and copies ran while one was open for 3% of the time, Pallas kernels for 0%

commit v1 on v0

v1 whole, which is shorter than its diff:
```python
import jax
import jax.numpy as jnp
from jax import lax
from jax.sharding import PartitionSpec as P


def swiglu_back(gate_pre, up_pre, hidden_grad):
    gate_f = gate_pre.astype(jnp.float32)
    up_f = up_pre.astype(jnp.float32)
    grad_f = hidden_grad.astype(jnp.float32)
    sigma = jax.nn.sigmoid(gate_f)
    gate_grad = (grad_f * up_f * sigma * (1.0 + gate_f * (1.0 - sigma))).astype(jnp.bfloat16)
    up_grad = (grad_f * gate_f * sigma).astype(jnp.bfloat16)
    return (gate_grad, up_grad)


def on_device(layer_input, gate_pre, up_pre, hidden_grad, gate_weight, up_weight):
    gate_loc, up_loc = swiglu_back(gate_pre, up_pre, hidden_grad)
    gate_grad = lax.all_gather(gate_loc, "row", axis=0, tiled=True)
    up_grad = lax.all_gather(up_loc, "row", axis=0, tiled=True)
    layer_x = lax.all_gather(layer_input, "col", axis=0, tiled=True)
    gate_part = lax.dot_general(
        layer_x, gate_grad, (((0,), (0,)), ((), ())), preferred_element_type=jnp.float32
    ).astype(jnp.bfloat16)
    gate_sum = lax.psum_scatter(gate_part, "depth", scatter_dimension=0, tiled=True)
    term = lax.dot_general(
        gate_grad, gate_weight, (((1,), (1,)), ((), ())), preferred_element_type=jnp.float32
    )
    term = term + lax.dot_general(
        up_grad, up_weight, (((1,), (1,)), ((), ())), preferred_element_type=jnp.float32
    )
    input_grad = lax.psum_scatter(term.astype(jnp.bfloat16), "col", scatter_dimension=0, tiled=True)
    up_part = lax.dot_general(
        layer_x, up_grad, (((0,), (0,)), ((), ())), preferred_element_type=jnp.float32
    ).astype(jnp.bfloat16)
    up_sum = lax.psum_scatter(up_part, "depth", scatter_dimension=0, tiled=True)
    return (input_grad, gate_sum, up_sum)


def solution(mesh):
    placed = (
        P(("depth", "col"), "row"),
        P(("depth", "row"), "col"),
        P(("depth", "row"), "col"),
        P(("depth", "row"), "col"),
        P("row", "col"),
        P("row", "col"),
    )
    return jax.shard_map(
        on_device,
        mesh=mesh,
        in_specs=placed,
        out_specs=(
            P(("depth", "col"), "row"),
            P(("row", "depth"), "col"),
            P(("row", "depth"), "col"),
        ),
        check_vma=False,
    )
```

time: 427 us -> 314 us (0.74)
  waiting for transfers between devices: 358 us -> 250 us
  other arithmetic: 16.2 us -> 2.55 us
  matrix products: 16.6 us -> 29 us
    all_gather x3 -> x2, waiting for transfers between devices: 331 us -> 212 us  [the longest x1 108 us: on_device(): up_grad = lax.all_gather(up_loc, 'row', axis=0, tiled=True)]
    unnamed x6 -> x7, waiting for transfers between devices: 2.23 us -> 37.1 us
    reduce_scatter x1, waiting for transfers between devices: 24.1 us -> 0.43 us  [on_device(): lax.psum_scatter(term.astype(jnp.bfloat16), 'col', scatter_dimension=0, t...]
    convert_element_type x1, other arithmetic: 16.1 us -> 2.55 us  [swiglu_back(): up_grad = (grad_f * gate_f * sigma).astype(jnp.bfloat16)]
  transfers between devices with their start and end apart: 5 -> 5, of which waited for: 5 -> 5; matrix products, arithmetic and copies ran while one was open for 3% -> 8% of each run, Pallas kernels for 0% -> 0%
where the time goes in v1:
time: 314 us; the launch traced here: 312 us
  waiting for transfers between devices  250 us (80%)
  matrix products  29 us (9%)
  between operations  13.8 us (4%)
  blocking collectives  13.2 us (4%)
  local copies, waits for them, and re-layouts  3.68 us (1%)
    all_gather x1, waiting for transfers between devices, on_device(): up_grad = lax.all_gather(up_loc, 'row', axis=0, tiled=True)  108 us
    all_gather x1, waiting for transfers between devices, on_device(): gate_grad = lax.all_gather(gate_loc, 'row', axis=0, tiled=True)  104 us
    unnamed x7, waiting for transfers between devices  37.1 us
    all_gather x1, blocking collectives, on_device(): layer_x = lax.all_gather(layer_input, 'col', axis=0, tiled=True)  13.2 us
    dot_general x1, matrix products, on_device(): lax.dot_general(up_grad, up_weight, (((1,), (1,)), ((), ())), preferred_e...  8.16 us
    dot_general x1, matrix products, on_device(): lax.dot_general(layer_x, up_grad, (((0,), (0,)), ((), ())), preferred_ele...  7.45 us
    dot_general x1, matrix products, on_device(): lax.dot_general(layer_x, gate_grad, (((0,), (0,)), ((), ())), preferred_e...  7.41 us
  transfers between devices with their start and end apart: 5, of which 5 were waited for; matrix products, arithmetic and copies ran while one was open for 8% of the time, Pallas kernels for 0%

profile of v1, /device:TPU:16, one launch (start us, length us, event | category | flops | bytes accessed | tf_op | source)
XLA Modules:
  0.0 311.9 jit_solution(3609781870868414459)
XLA Ops:
  7.2 0.0 copy-start
  7.2 0.0 all-gather.3.cloned.1.call-start
  7.2 2.5 fusion.11
  9.8 0.0 all-gather.3.cloned.1.call-update
  9.8 0.0 all-gather.5.cloned.1.call-start
  9.9 0.7 all-gather.5.cloned.1.call-update
  10.6 0.0 reduce-scatter.8.cloned.1.call-start
  10.6 13.2 %all_gather.11 = bf16[1536,128]{1,0:T(8,128)(2,1)S(1)} all-gather(bf16[384,128]{1,0:T(8,128)(2,1)} %param.6), channel_id=1, replica_groups=mesh['row'=32,'col'=4,'depth'=2] {'col'}, dimensions={0}, use_global_device_ids=true | all-gather | bytes 491520 | tf_op jit(solution)/shard_map/all_gather | solution.py:21
  23.8 103.9 %all-gather.3.cloned.1.call-done = bf16[1536,3696]{1,0:T(8,128)(2,1)} async-done(((bf16[48,3696]{1,0:T(8,128)(2,1)}), bf16[1536,3696]{1,0:T(8,128)(2,1)}) %all-gather.3.cloned.1.call-update) | async-done | bytes 11354128 | tf_op jit(solution)/shard_map/all_gather | solution.py:19
  127.7 6.0 %fusion.12 = f32[1536,128]{1,0:T(8,128)S(1)} fusion(bf16[1536,3696]{1,0:T(8,128)(2,1)} %all-gather.3.cloned.1.call-done, bf16[128,3696]{0,1:T(8,128)(2,1)S(1)} %copy-done), kind=kOutput, calls=%fused_computation.19 | convolution fusion | flops 1453326336 | bytes 13086720 | tf_op jit(solution)/shard_map/dot_general | solution.py:26
  133.7 108.0 %all-gather.5.cloned.1.call-done = bf16[1536,3696]{1,0:T(8,128)(2,1)} async-done(((bf16[48,3696]{1,0:T(8,128)(2,1)}), bf16[1536,3696]{1,0:T(8,128)(2,1)}) %all-gather.5.cloned.1.call-update) | async-done | bytes 11354128 | tf_op jit(solution)/shard_map/all_gather | solution.py:20
  241.7 8.2 %fusion.2 = bf16[1536,128]{1,0:T(8,128)(2,1)} fusion(f32[1536,128]{1,0:T(8,128)S(1)} %fusion.12, bf16[1536,3696]{1,0:T(8,128)(2,1)} %all-gather.5.cloned.1.call-done, bf16[128,3696]{0,1:T(8,128)(2,1)S(1)} %copy-done.1), kind=kOutput, calls=%fused_computation.5 | convolution fusion | flops 1453719552 | bytes 13479936 | tf_op jit(solution)/shard_map/dot_general | solution.py:29
  249.9 0.0 reduce-scatter.8.cloned.1.call-update
  249.9 0.0 reduce-scatter.10.cloned.1.call-start
  250.0 7.4 %fusion = bf16[128,3696]{0,1:T(8,128)(2,1)S(1)} fusion(bf16[1536,3696]{1,0:T(8,128)(2,1)} %all-gather.3.cloned.1.call-done, bf16[1536,128]{1,0:T(8,128)(2,1)S(1)} %all_gather.11), kind=kOutput, calls=%fused_computation.2 | convolution fusion | flops 1453799424 | bytes 12693504 | tf_op jit(solution)/shard_map/dot_general | solution.py:22
  257.4 1.8 copy.13
  259.2 0.0 reduce-scatter.10.cloned.1.call-update
  259.2 0.0 reduce-scatter.12.cloned.1.call-start
  259.3 7.5 %fusion.1 = bf16[128,3696]{0,1:T(8,128)(2,1)S(1)} fusion(bf16[1536,3696]{1,0:T(8,128)(2,1)} %all-gather.5.cloned.1.call-done, bf16[1536,128]{1,0:T(8,128)(2,1)S(1)} %all_gather.11), kind=kOutput, calls=%fused_computation.3 | convolution fusion | flops 1453799424 | bytes 12693504 | tf_op jit(solution)/shard_map/dot_general | solution.py:33
  266.7 1.8 copy.15
  268.6 0.0 reduce-scatter.12.cloned.1.call-update
  268.6 0.4 reduce-scatter.8.cloned.1.call-done
  269.0 18.2 %reduce-scatter.10.cloned.1.call-done = bf16[64,3696]{1,0:T(8,128)(2,1)} async-done(((bf16[128,3696]{1,0:T(8,128)(2,1)}), bf16[64,3696]{1,0:T(8,128)(2,1)}) %reduce-scatter.10.cloned.1.call-update) | async-done | bytes 473104
  287.2 18.2 %reduce-scatter.12.cloned.1.call-done = bf16[64,3696]{1,0:T(8,128)(2,1)} async-done(((bf16[128,3696]{1,0:T(8,128)(2,1)}), bf16[64,3696]{1,0:T(8,128)(2,1)}) %reduce-scatter.12.cloned.1.call-update) | async-done | bytes 473104
  (3 shorter events, 0.0 us)
Async XLA Ops:
  7.2 120.6 %copy-start = (bf16[128,3696]{0,1:T(8,128)(2,1)S(1)}, bf16[128,3696]{0,1:T(8,128)(2,1)}, u32[]{:S(2)}) copy-start(bf16[128,3696]{0,1:T(8,128)(2,1)} %param.10) | copy-start | bytes 2838532
  7.2 234.5 %copy-start.1 = (bf16[128,3696]{0,1:T(8,128)(2,1)S(1)}, bf16[128,3696]{0,1:T(8,128)(2,1)}, u32[]{:S(2)}) copy-start(bf16[128,3696]{0,1:T(8,128)(2,1)} %param.11) | copy-start | bytes 2838532
  7.2 120.5 %all-gather.3.cloned.1.call-start = ((), (), s32[]{:S(2)}) async-start(), calls=%async_computation.3 | async-start | bytes 11759616 | tf_op jit(solution)/shard_map/all_gather | solution.py:19
  9.8 231.9 %all-gather.5.cloned.1.call-start = ((), (), s32[]{:S(2)}) async-start(), calls=%async_computation.4 | async-start | bytes 11759616 | tf_op jit(solution)/shard_map/all_gather | solution.py:20
  10.6 258.5 %reduce-scatter.8.cloned.1.call-start = ((), (), s32[]{:S(2)}) async-start(), calls=%async_computation.5 | async-start | bytes 491520 | tf_op jit(solution)/shard_map/reduce_scatter | solution.py:32
  249.9 37.3 %reduce-scatter.10.cloned.1.call-start = ((), (), s32[]{:S(2)}) async-start(), calls=%async_computation.6 | async-start | bytes 1425408
  259.2 46.2 %reduce-scatter.12.cloned.1.call-start = ((), (), s32[]{:S(2)}) async-start(), calls=%async_computation.7 | async-start | bytes 1425408
Sparse Core Ops, SparseCore 0:
  11.2 116.4 all-gather.2
  130.9 110.7 all-gather.4
  250.0 18.9 reduce-scatter.7
  272.1 15.0 reduce-scatter.9
  290.3 15.0 reduce-scatter.11

commit v2 on v1

v2 whole, which is shorter than its diff:
```python
import jax
import jax.numpy as jnp
from jax import lax
from jax.experimental import pallas as pl
from jax.experimental.pallas import tpu as pltpu
from jax.sharding import PartitionSpec as P

NX, NY, NZ, NC = 4, 4, 8, 2
ROWS = 48
ZB = NX * ROWS
LAYER = NZ * ZB
UNITS = 3696
XB = 1920
WIDE = 128
DB = NX * WIDE
TB = 2 * ZB
HALF = WIDE // 2
CHUNKS = (640, 640, 640)
STARTS = (0, 640, 1280)
N_COPIES = 104
BF, F32 = jnp.bfloat16, jnp.float32

PIECES = (
    (0, 0, 0, 0, 1920),
    (0, 1920, 1, 0, 1776),
    (1, 0, 1, 1792, 128),
    (1, 128, 2, 0, 1920),
    (1, 2048, 3, 0, 1648),
)
PADS = ((1, 1664, 1792), (3, 1536, 1920))


def kernel(
    x_ref, gate_ref, up_ref, grad_ref, gw_ref, uw_ref,
    ig_ref, go_ref, uo_ref,
    own_g, g0, g1, g2, own_w, w_all, xt_own, xt, part, part_in, summed, summed_in,
    wp0, wp1, wp2, wr0, wr1, wr2, ws0, ws1, ws2, w_out,
    send_sem, recv_sem, local_sem,
):
    row, y, c = lax.axis_index("row"), lax.axis_index("col"), lax.axis_index("depth")
    z, x = row // NX, lax.rem(row, NX)
    g, wp, wr, ws = (g0, g1, g2), (wp0, wp1, wp2), (wr0, wr1, wr2), (ws0, ws1, ws2)
    last = len(CHUNKS) - 1

    def at(x_=x, y_=y, z_=z, c_=c):
        return (z_ * NX + x_, y_, c_)

    def turn(value, by, n):
        return lax.rem(value + (by + n), n)

    sends, locals_ = [], []

    def send(src, dst, device):
        i = len(sends)
        copy = pltpu.make_async_remote_copy(
            src_ref=src, dst_ref=dst, send_sem=send_sem.at[i], recv_sem=recv_sem.at[i],
            device_id=device, device_id_type=pl.DeviceIdType.MESH,
        )
        copy.start()
        sends.append(copy)
        return copy

    def local(src, dst):
        copy = pltpu.make_async_copy(src, dst, local_sem.at[len(locals_)])
        copy.start()
        locals_.append(copy)
        return copy

    partners = [at(x_=turn(x, o, NX)) for o in (1, 2, 3)]
    partners += [at(y_=turn(y, o, NY)) for o in (1, 2, 3)]
    partners += [at(z_=turn(z, o, NZ)) for o in (1, -1)]
    partners += [at(c_=1 - c)]
    barrier = pltpu.get_barrier_semaphore()
    for device in partners:
        pl.semaphore_signal(barrier, inc=1, device_id=device, device_id_type=pl.DeviceIdType.MESH)

    for block, first, end in PADS:
        own_g[block, :, first:end] = jnp.zeros((ROWS, end - first), BF)
    for which, first, block, there, columns in PIECES:
        for lo in range(0, columns, WIDE):
            n = min(WIDE, columns - lo)
            cut = slice(first + lo, first + lo + n)
            gate = gate_ref[:, cut].astype(F32)
            grad = grad_ref[:, cut].astype(F32)
            sigma = 1.0 / (1.0 + jnp.exp(-gate))
            if which == 0:
                value = grad * up_ref[:, cut].astype(F32) * sigma * (1.0 + gate * (1.0 - sigma))
            else:
                value = grad * gate * sigma
            own_g[block, :, there + lo:there + lo + n] = value.astype(BF)
    xt_own[...] = x_ref[...].astype(F32).T.astype(BF)

    pl.semaphore_wait(barrier, len(partners))

    mine = pl.ds(pl.multiple_of(row * ROWS, 16), ROWS)
    swapped = []

    def swap(k):
        cols = pl.ds(STARTS[k], CHUNKS[k])
        copies = []
        for o in (1, 2, 3):
            to = turn(x, o, NX)
            copies.append(send(own_g.at[to, :, cols], g[k].at[mine], at(x_=to)))
        swapped.append((copies, local(own_g.at[x, :, cols], g[k].at[mine])))

    swap(0)
    xt_rows = pl.ds(pl.multiple_of(x * WIDE, WIDE), WIDE)
    xt_cols = pl.ds(pl.multiple_of(y * TB, 128), TB)
    xt_x = [send(xt_own, xt.at[xt_rows, xt_cols], at(x_=turn(x, o, NX))) for o in (1, 2, 3)]
    xt_local = local(xt_own, xt.at[xt_rows, xt_cols])
    swap(1)

    for block, first, end in PADS:
        own_w[block, :, first:end] = jnp.zeros((WIDE, end - first), BF)
    for which, first, block, there, columns in PIECES:
        source = (gw_ref, uw_ref)[which]
        own_w[block, :, there:there + columns] = source[:, first:first + columns]

    def arrived(k):
        copies, copy = swapped[k]
        for remote in copies:
            remote.wait_recv()
        copy.wait()

    ring = {
        1: [(1, 0), (1, 1), (2, 0), (2, 1), (3, 0), (3, 1), (4, 0)],
        -1: [(1, 1), (1, 0), (2, 1), (2, 0), (3, 1), (3, 0), (4, 1)],
    }
    events = len(ring[1])
    moved = {(k, way): [] for k in range(len(CHUNKS)) for way in (1, -1)}

    def pass_on(k, e, way):
        if e >= events:
            k, e = k + 1, e - events
        if k > last:
            return
        hop, half = ring[way][e]
        block = turn(z, -way * (hop - 1), NZ)
        rows = pl.ds(pl.multiple_of(block * ZB + half * (ZB // 2), 16), ZB // 2)
        moved[k, way].append(send(g[k].at[rows], g[k].at[rows], at(z_=turn(z, way, NZ))))

    arrived(0)
    for e in (0, 1):
        for way in (1, -1):
            pass_on(0, e, way)
    swap(2)
    w_rows = pl.ds(pl.multiple_of(x * WIDE, WIDE), WIDE)
    w_sent = [
        send(own_w.at[turn(x, o, NX)], w_all.at[w_rows], at(x_=turn(x, o, NX))) for o in (1, 2, 3)
    ]
    w_local = local(own_w.at[x], w_all.at[w_rows])
    for copy in xt_x:
        copy.wait_recv()
    xt_local.wait()
    xt_y = [send(xt.at[:, xt_cols], xt.at[:, xt_cols], at(y_=turn(y, o, NY))) for o in (1, 2, 3)]

    def weight_piece(k, lo):
        n = min(256, CHUNKS[k] - lo)
        value = jnp.dot(xt[...], g[k][:, lo:lo + n], preferred_element_type=F32).astype(BF)
        for b in range(NX):
            for h in range(NC):
                wp[k][h, b * HALF:(b + 1) * HALF, lo:lo + n] = value[
                    b * WIDE + h * HALF:b * WIDE + (h + 1) * HALF
                ]

    exchanged = {}

    def exchange(k):
        exchanged[k] = send(wp[k].at[1 - c], wr[k], at(c_=1 - c))

    returned = []

    def give_back(k):
        exchanged[k].wait_recv()
        ws[k][...] = (wp[k][c].astype(F32) + wr[k][...].astype(F32)).astype(BF)
        cols = pl.ds(STARTS[k], CHUNKS[k])

        def rows(of):
            return pl.ds(pl.multiple_of(of * HALF, HALF), HALF)

        for o in (1, 2, 3):
            to = turn(x, o, NX)
            returned.append(send(ws[k].at[rows(to)], w_out.at[x, :, cols], at(x_=to)).wait_recv)
        returned.append(local(ws[k].at[rows(x)], w_out.at[x, :, cols]).wait)

    partial = {}

    def rows_of(b):
        return pl.ds(pl.multiple_of(turn(z, b, NZ) * ZB, 64), ZB)

    def input_part(b):
        rows = rows_of(b)
        total = None
        for k in range(len(CHUNKS)):
            term = lax.dot_general(
                g[k][rows, :], w_all[:, STARTS[k]:STARTS[k] + CHUNKS[k]],
                (((1,), (1,)), ((), ())), preferred_element_type=F32,
            )
            total = term if total is None else total + term
        for b_ in range(NX):
            part[b_, rows, :] = total[:, b_ * WIDE:(b_ + 1) * WIDE].astype(BF)
        partial[b] = [
            send(part.at[turn(x, o, NX), rows], part_in.at[o - 1, rows], at(x_=turn(x, o, NX)))
            for o in (1, 2, 3)
        ]

    def input_sum(b):
        rows = rows_of(b)
        for copy in partial[b]:
            copy.wait_recv()
        total = part[x, rows, :].astype(F32)
        for o in range(3):
            total = total + part_in[o, rows, :].astype(F32)
        summed[rows, :] = total.astype(BF)

    for k in range(len(CHUNKS)):
        for e in range(events):
            if e == events - 2 and k < last:
                arrived(k + 1)
            for way in (1, -1):
                moved[k, way][e].wait_recv()
                pass_on(k, e + 2, way)
            if k == 1 and e == 0:
                for copy in xt_y:
                    copy.wait_recv()
            if k >= 1:
                if e * 256 < CHUNKS[k - 1]:
                    weight_piece(k - 1, e * 256)
                if e == 3:
                    exchange(k - 1)
                if e == 5:
                    give_back(k - 1)
            if k == last:
                if e == 0:
                    for copy in w_sent:
                        copy.wait_recv()
                    w_local.wait()
                for b in ((0,), (-1,), (1,), (-2,), (2,), (-3, 3), (4,))[e]:
                    input_part(b)
                for b in ((), (), (0,), (-1,), (1,), (-2,), (2,))[e]:
                    input_sum(b)

    for lo in range(0, CHUNKS[last], 256):
        weight_piece(last, lo)
    exchange(last)
    for b in (-3, 3, 4):
        input_sum(b)

    def tokens(of):
        return pl.ds(pl.multiple_of(of * TB, 128), TB)

    over_y = [
        send(summed.at[tokens(turn(y, o, NY))], summed_in.at[o - 1], at(y_=turn(y, o, NY)))
        for o in (1, 2, 3)
    ]
    give_back(last)
    for copy in over_y:
        copy.wait_recv()
    total = summed[tokens(y), :].astype(F32)
    for o in range(3):
        total = total + summed_in[o].astype(F32)
    ig_ref[...] = total.astype(BF)

    for wait in returned:
        wait()
    for which, first, block, there, columns in PIECES:
        target = (go_ref, uo_ref)[which]
        target[:, first:first + columns] = w_out[block, :, there:there + columns]
    for copy in sends:
        copy.wait_send()


def on_device(layer_input, gate_pre, up_pre, hidden_grad, gate_weight, up_weight):
    vmem = pltpu.VMEM
    scratch = [vmem((NX, ROWS, XB), BF)]
    scratch += [vmem((LAYER, w), BF) for w in CHUNKS]
    scratch += [
        vmem((NX, WIDE, XB), BF),
        vmem((DB, XB), BF),
        vmem((WIDE, TB), BF),
        vmem((DB, LAYER), BF),
        vmem((NX, LAYER, WIDE), BF),
        vmem((NX - 1, LAYER, WIDE), BF),
        vmem((LAYER, WIDE), BF),
        vmem((NY - 1, TB, WIDE), BF),
    ]
    scratch += [vmem((NC, NX * HALF, w), BF) for w in CHUNKS]
    scratch += [vmem((NX * HALF, w), BF) for w in CHUNKS]
    scratch += [vmem((NX * HALF, w), BF) for w in CHUNKS]
    scratch += [vmem((NX, HALF, XB), BF)]
    scratch += [
        pltpu.SemaphoreType.DMA((N_COPIES,)),
        pltpu.SemaphoreType.DMA((N_COPIES,)),
        pltpu.SemaphoreType.DMA((8,)),
    ]
    in_vmem = pl.BlockSpec(memory_space=pltpu.VMEM)
    return pl.pallas_call(
        kernel,
        out_shape=(
            jax.ShapeDtypeStruct((TB, WIDE), BF),
            jax.ShapeDtypeStruct((HALF, UNITS), BF),
            jax.ShapeDtypeStruct((HALF, UNITS), BF),
        ),
        in_specs=[in_vmem] * 6,
        out_specs=(in_vmem,) * 3,
        scratch_shapes=scratch,
        compiler_params=pltpu.CompilerParams(
            collective_id=0, has_side_effects=True, vmem_limit_bytes=56 * 1024 * 1024
        ),
    )(layer_input, gate_pre, up_pre, hidden_grad, gate_weight, up_weight)


def solution(mesh):
    placed = (
        P(("depth", "col"), "row"),
        P(("depth", "row"), "col"),
        P(("depth", "row"), "col"),
        P(("depth", "row"), "col"),
        P("row", "col"),
        P("row", "col"),
    )
    return jax.shard_map(
        on_device,
        mesh=mesh,
        in_specs=placed,
        out_specs=(
            P(("depth", "col"), "row"),
            P(("row", "depth"), "col"),
            P(("row", "depth"), "col"),
        ),
        check_vma=False,
    )
```

time: 314 us -> 101 us (0.32)
  waiting for transfers between devices: 250 us -> 0 us
  Pallas kernels: 0 us -> 91.4 us
  matrix products: 29 us -> 0 us
  blocking collectives: 13.2 us -> 0 us
  between operations: 13.8 us -> 0.65 us
  local copies, waits for them, and re-layouts: 3.68 us -> 8.36 us
    all_gather x2 -> x0, waiting for transfers between devices: 212 us -> none  [the longest x1 108 us: on_device(): up_grad = lax.all_gather(up_loc, 'row', axis=0, tiled=True)]
    pallas_call x0 -> x1, Pallas kernels: none -> 91.4 us  [on_device(): pl.pallas_call(kernel, out_shape=(jax.ShapeDtypeStruct((TB, WIDE), BF), j...]
    unnamed x7 -> x0, waiting for transfers between devices: 37.1 us -> none
    dot_general x4 -> x0, matrix products: 29 us -> none  [the longest x1 8.16 us: on_device(): lax.dot_general(up_grad, up_weight, (((1,), (1,)), ((), ())), preferred_e...]
    all_gather x1 -> x0, blocking collectives: 13.2 us -> none  [on_device(): layer_x = lax.all_gather(layer_input, 'col', axis=0, tiled=True)]
    unnamed x6 -> x9, local copies, waits for them, and re-layouts: 3.68 us -> 8.36 us
  transfers between devices with their start and end apart: 5 -> 0, of which waited for: 5 -> 0; matrix products, arithmetic and copies ran while one was open for 8% -> 0% of each run, Pallas kernels for 0% -> 0%
where the time goes in v2:
time: 101 us; the launch traced here: 100 us
  Pallas kernels  91.4 us (90%)
  local copies, waits for them, and re-layouts  8.36 us (8%)
    pallas_call x1, Pallas kernels, on_device(): pl.pallas_call(kernel, out_shape=(jax.ShapeDtypeStruct((TB, WIDE), BF), j...  91.4 us
    unnamed x9, local copies, waits for them, and re-layouts  8.36 us

profile of v2, /device:TPU:16, one launch (start us, length us, event | category | flops | bytes accessed | tf_op | source)
XLA Modules:
  0.0 100.4 jit_solution(1939947174359717646)
XLA Ops:
  0.6 0.0 copy-start
  0.6 2.3 %copy.9.gw_ref = bf16[128,3696]{1,0:T(8,128)(2,1)} copy(bf16[128,3696]{0,1:T(8,128)(2,1)} %param.10) | data formatting | bytes 1892352 | tf_op args[4]
  3.0 0.0 copy-done
  3.0 1.8 %copy.10.uw_ref = bf16[128,3696]{1,0:T(8,128)(2,1)} copy(bf16[128,3696]{0,1:T(8,128)(2,1)S(1)} %copy-done) | data formatting | bytes 1892352 | tf_op args[5]
  4.8 91.4 %shard_map.85 = (bf16[384,128]{1,0:T(8,128)(2,1)}, bf16[64,3696]{1,0:T(8,128)(2,1)}, bf16[64,3696]{1,0:T(8,128)(2,1)}) custom-call(bf16[384,128]{1,0:T(8,128)(2,1)} %x_ref.1, bf16[48,3696]{1,0:T(8,128)(2,1)} %gate_ref.1, bf16[48,3696]{1,0:T(8,128)(2,1)} %up_ref.1, bf16[48,3696]{1,0:T(8,128)(2,1)} %grad_ref.1, bf16[128,3696]{1,0:T(8,128)(2,1)} %copy.9.gw_ref, ...), custom_call_target="tpu_custom_call" | custom-call | tf_op jit(solution)/shard_map/pallas_call | solution.py:297
  96.2 1.5 %copy.14 = bf16[384,128]{1,0:T(8,128)(2,1)} copy(bf16[384,128]{1,0:T(8,128)(2,1)} %get-tuple-element.6) | data formatting | bytes 196608
  97.8 0.0 copy-start.1
  97.8 1.9 %copy.15 = bf16[64,3696]{1,0:T(8,128)(2,1)} copy(bf16[64,3696]{1,0:T(8,128)(2,1)} %get-tuple-element.7) | data formatting | bytes 946176
  99.7 0.0 copy-done.1
  99.7 0.8 copy.16
Async XLA Ops:
  0.6 2.3 %copy-start = (bf16[128,3696]{0,1:T(8,128)(2,1)S(1)}, bf16[128,3696]{0,1:T(8,128)(2,1)}, u32[]{:S(2)}) copy-start(bf16[128,3696]{0,1:T(8,128)(2,1)} %param.11) | copy-start | bytes 2838532
  97.8 1.9 %copy-start.1 = (bf16[64,3696]{1,0:T(8,128)(2,1)S(1)}, bf16[64,3696]{1,0:T(8,128)(2,1)}, u32[]{:S(2)}) copy-start(bf16[64,3696]{1,0:T(8,128)(2,1)} %get-tuple-element.8) | copy-start | bytes 1419268

commit v3 on v2

v3 whole, which is shorter than its diff:
```python
import jax
import jax.numpy as jnp
from jax import lax
from jax.experimental import pallas as pl
from jax.experimental.pallas import tpu as pltpu
from jax.sharding import PartitionSpec as P

NX, NY, NZ, NC = 4, 4, 8, 2
ROWS = 48
ZB = NX * ROWS
LAYER = NZ * ZB
UNITS = 3696
XB = 1920
TILES = 29
WIDE = 128
DB = NX * WIDE
TB = 2 * ZB
HALF = WIDE // 2
CHUNKS = (640, 640, 640)
STARTS = (0, 640, 1280)
N_COPIES = 112
BF, F32 = jnp.bfloat16, jnp.float32

PIECES = (
    (0, 0, 0, 0, 1920),
    (0, 1920, 1, 0, 1776),
    (1, 0, 1, 1792, 128),
    (1, 128, 2, 0, 1920),
    (1, 2048, 3, 0, 1648),
)
PADS = ((1, 1664, 1792), (3, 1536, 1920))
ROW_PADS = ((1, 1776, 1792), (3, 1648, 1920))


def kernel(
    x_hbm, gate_hbm, up_hbm, grad_hbm, gw_hbm, uw_hbm,
    ig_ref, w_out,
    x_ref, gate_ref, up_ref, grad_ref, own_g, g0, g1, g2, own_w, w_all, xt_own, xt, part, part_in, summed, summed_in,
    wp0, wp1, wp2, wr0, wr1, wr2, ws0, ws1, ws2,
    send_sem, recv_sem, local_sem, y_send, y_recv,
):
    row, y, c = lax.axis_index("row"), lax.axis_index("col"), lax.axis_index("depth")
    z, x = row // NX, lax.rem(row, NX)
    g, wp, wr, ws = (g0, g1, g2), (wp0, wp1, wp2), (wr0, wr1, wr2), (ws0, ws1, ws2)
    last = len(CHUNKS) - 1

    def at(x_=x, y_=y, z_=z, c_=c):
        return (z_ * NX + x_, y_, c_)

    def turn(value, by, n):
        return lax.rem(value + (by + n), n)

    sends, locals_ = [], []

    def send(src, dst, device):
        i = len(sends)
        copy = pltpu.make_async_remote_copy(
            src_ref=src, dst_ref=dst, send_sem=send_sem.at[i], recv_sem=recv_sem.at[i],
            device_id=device, device_id_type=pl.DeviceIdType.MESH,
        )
        copy.start()
        sends.append(copy)
        return copy

    def local(src, dst):
        copy = pltpu.make_async_copy(src, dst, local_sem.at[len(locals_)])
        copy.start()
        locals_.append(copy)
        return copy

    partners = [at(x_=turn(x, o, NX)) for o in (1, 2, 3)]
    partners += [at(y_=turn(y, o, NY)) for o in (1, 2, 3)]
    partners += [at(z_=turn(z, o, NZ)) for o in (1, -1)]
    partners += [at(c_=1 - c)]
    barrier = pltpu.get_barrier_semaphore()
    for device in partners:
        pl.semaphore_signal(barrier, inc=1, device_id=device, device_id_type=pl.DeviceIdType.MESH)

    loads = [
        local(src, dst)
        for src, dst in ((gate_hbm, gate_ref), (up_hbm, up_ref), (grad_hbm, grad_ref), (x_hbm, x_ref))
    ]
    w_loads = [
        local(
            (gw_hbm, uw_hbm)[which].at[pl.ds(first, columns)],
            own_w.at[block, pl.ds(there, columns)],
        )
        for which, first, block, there, columns in PIECES
    ]
    for block, first, end in ROW_PADS:
        own_w[block, first:end, :] = jnp.zeros((end - first, WIDE), BF)
    for block, first, end in PADS:
        own_g[block, :, first:end] = jnp.zeros((ROWS, end - first), BF)
    for load in loads[:3]:
        load.wait()

    done = set()

    def gated(k):
        for t in range(TILES):
            chunks = [(tile % (XB // WIDE)) * WIDE // CHUNKS[0] for tile in (t, TILES + t)]
            if k not in chunks or t in done:
                continue
            done.add(t)
            n = min(WIDE, UNITS - t * WIDE)
            cut = slice(t * WIDE, t * WIDE + n)
            gate = gate_ref[:, cut].astype(F32)
            grad = grad_ref[:, cut].astype(F32)
            sigma = 1.0 / (1.0 + jnp.exp(-gate))
            scaled = grad * sigma
            values = (
                scaled * up_ref[:, cut].astype(F32) * (1.0 + gate * (1.0 - sigma)), scaled * gate
            )
            for tile, value in zip((t, TILES + t), values):
                block, first = divmod(tile * WIDE, XB)
                own_g[block, :, first:first + n] = value.astype(BF)

    gated(0)
    pl.semaphore_wait(barrier, len(partners))

    def slab(of):
        return pl.ds(pl.multiple_of((z * NX + of) * ROWS, 16), ROWS)

    mates = {1: x + 1 - 2 * lax.rem(x, 2), 2: turn(x, 2, NX), 3: 3 - x}
    swapped, first_hop = [], {}

    def swap(k):
        cols = pl.ds(STARTS[k], CHUNKS[k])
        for way in (1, -1):
            first_hop[k, way] = send(
                own_g.at[x, :, cols], g[k].at[slab(x)], at(z_=turn(z, way, NZ))
            )
        copies = {}
        for m in (1, 3, 2):
            copies[m] = send(own_g.at[mates[m], :, cols], g[k].at[slab(x)], at(x_=mates[m]))
        swapped.append((copies, local(own_g.at[x, :, cols], g[k].at[slab(x)])))

    def arrived(k):
        copies, copy = swapped[k]
        for m in (1, 2, 3):
            copies[m].wait_recv()
        copy.wait()

    near, far = [(h, s) for h in (1, 2, 3) for s in (0, 1)], [(h, s) for h in (1, 2, 3) for s in (1, 0)]
    items = {1: [], -1: [(0, h, s) for h, s in near]}
    for k in range(len(CHUNKS)):
        items[1] += [(k, h, s) for h, s in near + [(4, 0)]]
        if k:
            items[-1] += [(k, h, s) for h, s in far + [(4, 1)]]
    items[-1].insert(7, (0, 4, 1))
    events = 7
    moved = {1: [], -1: []}

    def pass_on(i, way):
        if i >= len(items[way]):
            return
        k, hop, half = items[way][i]
        to = at(z_=turn(z, way, NZ))
        if (hop, half) == (1, 0):
            rows = slab(mates[1])
            moved[way].append((first_hop[k, way], send(g[k].at[rows], g[k].at[rows], to)))
            return
        block = turn(z, -way * (hop - 1), NZ)
        part_ = x // 2 if half == 0 else 1 - x // 2
        rows = pl.ds(pl.multiple_of(block * ZB + part_ * (ZB // 2), 16), ZB // 2)
        moved[way].append((send(g[k].at[rows], g[k].at[rows], to),))

    swap(0)
    gated(1)
    swap(1)
    swapped[0][0][1].wait_recv()
    for way in (1, -1):
        pass_on(0, way)
    gated(2)
    swap(2)
    for m in (2, 3):
        swapped[0][0][m].wait_recv()
    swapped[0][1].wait()
    for way in (1, -1):
        pass_on(1, way)
    loads[3].wait()
    xt_own[...] = x_ref[...].astype(F32).T.astype(BF)
    xt_rows = pl.ds(pl.multiple_of(x * WIDE, WIDE), WIDE)
    xt_cols = pl.ds(pl.multiple_of(y * TB, 128), TB)
    xt_x = [send(xt_own, xt.at[xt_rows, xt_cols], at(x_=turn(x, o, NX))) for o in (1, 2, 3)]
    xt_local = local(xt_own, xt.at[xt_rows, xt_cols])
    for load in w_loads:
        load.wait()

    w_half = pl.ds(pl.multiple_of(c * (XB // 2), 64), XB // 2)
    w_cols = pl.ds(pl.multiple_of(x * WIDE, WIDE), WIDE)
    w_sent = [
        send(
            own_w.at[turn(x, o, NX), w_half], w_all.at[w_half, w_cols], at(x_=turn(x, o, NX))
        )
        for o in (1, 2, 3)
    ]
    w_local = local(own_w.at[x, w_half], w_all.at[w_half, w_cols])
    for copy in xt_x:
        copy.wait_recv()
    xt_local.wait()
    xt_y = [send(xt.at[:, xt_cols], xt.at[:, xt_cols], at(y_=turn(y, o, NY))) for o in (1, 2, 3)]

    def weight_piece(k, lo):
        n = min(256, CHUNKS[k] - lo)
        value = jnp.dot(xt[...], g[k][:, lo:lo + n], preferred_element_type=F32).astype(BF)
        for b in range(NX):
            for h in range(NC):
                wp[k][h, b * HALF:(b + 1) * HALF, lo:lo + n] = value[
                    b * WIDE + h * HALF:b * WIDE + (h + 1) * HALF
                ]

    exchanged = {}

    def exchange(k):
        exchanged[k] = send(wp[k].at[1 - c], wr[k], at(c_=1 - c))

    returned = []

    def give_back(k):
        exchanged[k].wait_recv()
        ws[k][...] = (wp[k][c].astype(F32) + wr[k][...].astype(F32)).astype(BF)
        cols = pl.ds(STARTS[k], CHUNKS[k])

        def rows(of):
            return pl.ds(pl.multiple_of(of * HALF, HALF), HALF)

        for o in (1, 2, 3):
            to = turn(x, o, NX)
            returned.append(send(ws[k].at[rows(to)], w_out.at[x, :, cols], at(x_=to)).wait_recv)
        returned.append(local(ws[k].at[rows(x)], w_out.at[x, :, cols]).wait)

    partial, scattered = {}, []

    def rows_of(b):
        return pl.ds(pl.multiple_of(turn(z, b, NZ) * ZB, 64), ZB)

    def input_part(b):
        rows = rows_of(b)
        total = None
        for k in range(len(CHUNKS)):
            term = jnp.dot(
                g[k][rows, :], w_all[STARTS[k]:STARTS[k] + CHUNKS[k], :],
                preferred_element_type=F32,
            )
            total = term if total is None else total + term
        for b_ in range(NX):
            part[b_, rows, :] = total[:, b_ * WIDE:(b_ + 1) * WIDE].astype(BF)
        partial[b] = [
            send(part.at[turn(x, o, NX), rows], part_in.at[o - 1, rows], at(x_=turn(x, o, NX)))
            for o in (1, 2, 3)
        ]

    def input_sum(b):
        rows = rows_of(b)
        for copy in partial[b]:
            copy.wait_recv()
        total = part[x, rows, :].astype(F32)
        for o in range(3):
            total = total + part_in[o, rows, :].astype(F32)
        summed[rows, :] = total.astype(BF)
        block = turn(z, b, NZ)
        owner, parity = block // 2, lax.rem(block, 2)
        away = turn(owner - y, 0, NY)
        copy = pltpu.make_async_remote_copy(
            src_ref=summed.at[rows],
            dst_ref=summed_in.at[lax.rem(away + 3, NY), pl.ds(pl.multiple_of(parity * ZB, 64), ZB)],
            send_sem=y_send.at[b + 3], recv_sem=y_recv.at[2 * away + parity],
            device_id=at(y_=owner), device_id_type=pl.DeviceIdType.MESH,
        )
        scattered.append((away, copy))

        @pl.when(away != 0)
        def _():
            copy.start()

    over_core = []
    parts_at = {(1, 6): (0,), (2, 1): (-1, 1), (2, 3): (-2, 2), (2, 5): (-3, 3), (2, 6): (4,)}
    sums_at = {(2, 1): (0,), (2, 4): (-1, 1), (2, 6): (-2, 2)}
    for k in range(len(CHUNKS)):
        for e in range(events):
            if e == 4 and k < last:
                arrived(k + 1)
            for way in (1, -1):
                for copy in moved[way][k * events + e]:
                    copy.wait_recv()
                pass_on(k * events + e + 2, way)
            if (k, e) == (1, 0):
                for copy in xt_y:
                    copy.wait_recv()
            if (k, e) == (1, 4):
                for copy in w_sent:
                    copy.wait_recv()
                w_local.wait()
                over_core.append(send(w_all.at[w_half], w_all.at[w_half], at(c_=1 - c)))
            if (k, e) == (1, 6):
                over_core[0].wait_recv()
            for b in parts_at.get((k, e), ()):
                input_part(b)
            if k >= 1:
                if e < 3 and e * 256 < CHUNKS[k - 1]:
                    weight_piece(k - 1, e * 256)
                if e == 2:
                    exchange(k - 1)
                if e == 4:
                    give_back(k - 1)
            for b in sums_at.get((k, e), ()):
                input_sum(b)

    for lo in range(0, CHUNKS[last], 256):
        weight_piece(last, lo)
    exchange(last)
    for b in (-3, 3, 4):
        input_sum(b)
    give_back(last)

    for o in (1, 2, 3):
        for parity in (0, 1):
            landed = summed_in.at[o - 1, pl.ds(parity * ZB, ZB)]
            pltpu.make_async_remote_copy(
                src_ref=landed, dst_ref=landed,
                send_sem=y_send.at[0], recv_sem=y_recv.at[2 * o + parity],
                device_id=at(y_=turn(y, o, NY)), device_id_type=pl.DeviceIdType.MESH,
            ).wait_recv()
    total = summed[pl.ds(pl.multiple_of(y * TB, 128), TB), :].astype(F32)
    for o in range(3):
        total = total + summed_in[o].astype(F32)
    ig_ref[...] = total.astype(BF)

    for wait in returned:
        wait()
    for copy in sends:
        copy.wait_send()
    for away, copy in scattered:
        pl.when(away != 0)(copy.wait_send)


def unpack(ig_in, w_out, ig_ref, go_ref, uo_ref):
    ig_ref[...] = ig_in[...]
    for which, first, block, there, columns in PIECES:
        target = (go_ref, uo_ref)[which]
        target[:, first:first + columns] = w_out[block, :, there:there + columns]


def on_device(layer_input, gate_pre, up_pre, hidden_grad, gate_weight, up_weight):
    vmem = pltpu.VMEM
    scratch = [vmem((TB, WIDE), BF)] + [vmem((ROWS, UNITS), BF)] * 3 + [vmem((NX, ROWS, XB), BF)]
    scratch += [vmem((LAYER, w), BF) for w in CHUNKS]
    scratch += [
        vmem((NX, XB, WIDE), BF),
        vmem((XB, DB), BF),
        vmem((WIDE, TB), BF),
        vmem((DB, LAYER), BF),
        vmem((NX, LAYER, WIDE), BF),
        vmem((NX - 1, LAYER, WIDE), BF),
        vmem((LAYER, WIDE), BF),
        vmem((NY, TB, WIDE), BF),
    ]
    scratch += [vmem((NC, NX * HALF, w), BF) for w in CHUNKS]
    scratch += [vmem((NX * HALF, w), BF) for w in CHUNKS]
    scratch += [vmem((NX * HALF, w), BF) for w in CHUNKS]
    scratch += [
        pltpu.SemaphoreType.DMA((N_COPIES,)),
        pltpu.SemaphoreType.DMA((N_COPIES,)),
        pltpu.SemaphoreType.DMA((20,)),
        pltpu.SemaphoreType.DMA((NZ,)),
        pltpu.SemaphoreType.DMA((2 * NY,)),
    ]
    in_vmem = pl.BlockSpec(memory_space=pltpu.VMEM)
    anywhere = pl.BlockSpec(memory_space=pl.ANY)
    input_grad, packed = pl.pallas_call(
        kernel,
        out_shape=(
            jax.ShapeDtypeStruct((TB, WIDE), BF),
            jax.ShapeDtypeStruct((NX, HALF, XB), BF),
        ),
        in_specs=[anywhere] * 6,
        out_specs=(in_vmem, anywhere),
        scratch_shapes=scratch,
        compiler_params=pltpu.CompilerParams(
            collective_id=0, has_side_effects=True, vmem_limit_bytes=56 * 1024 * 1024
        ),
    )(layer_input, gate_pre, up_pre, hidden_grad, gate_weight.T, up_weight.T)
    return pl.pallas_call(
        unpack,
        out_shape=(
            jax.ShapeDtypeStruct((TB, WIDE), BF),
            jax.ShapeDtypeStruct((HALF, UNITS), BF),
            jax.ShapeDtypeStruct((HALF, UNITS), BF),
        ),
        in_specs=[in_vmem] * 2,
        out_specs=(in_vmem,) * 3,
    )(input_grad, packed)


def solution(mesh):
    placed = (
        P(("depth", "col"), "row"),
        P(("depth", "row"), "col"),
        P(("depth", "row"), "col"),
        P(("depth", "row"), "col"),
        P("row", "col"),
        P("row", "col"),
    )
    return jax.shard_map(
        on_device,
        mesh=mesh,
        in_specs=placed,
        out_specs=(
            P(("depth", "col"), "row"),
            P(("row", "depth"), "col"),
            P(("row", "depth"), "col"),
        ),
        check_vma=False,
    )
```

time: 101 us -> 97.1 us (0.961)
  local copies, waits for them, and re-layouts: 8.36 us -> 0 us
  Pallas kernels: 91.4 us -> 94.9 us
    unnamed x9 -> x0, local copies, waits for them, and re-layouts: 8.36 us -> none
    pallas_call x0 -> x1, Pallas kernels: none -> 2.26 us  [on_device(): pl.pallas_call(unpack, out_shape=(jax.ShapeDtypeStruct((TB, WIDE), BF), j...]
    pallas_call x1, Pallas kernels: 91.4 us -> 92.7 us  [on_device(): pl.pallas_call(kernel, out_shape=(jax.ShapeDtypeStruct((TB, WIDE), BF), j...]
where the time goes in v3:
time: 97.1 us; the launch traced here: 95.6 us
  Pallas kernels  94.9 us (98%)
    pallas_call x1, Pallas kernels, on_device(): pl.pallas_call(kernel, out_shape=(jax.ShapeDtypeStruct((TB, WIDE), BF), j...  92.7 us
    pallas_call x1, Pallas kernels, on_device(): pl.pallas_call(unpack, out_shape=(jax.ShapeDtypeStruct((TB, WIDE), BF), j...  2.26 us

profile of v3, /device:TPU:16, one launch (start us, length us, event | category | flops | bytes accessed | tf_op | source)
XLA Modules:
  0.0 95.6 jit_solution(2041727343289088005)
XLA Ops:
  0.6 92.7 %shard_map.85 = (bf16[384,128]{1,0:T(8,128)(2,1)}, bf16[4,64,1920]{2,1,0:T(8,128)(2,1)}) custom-call(bf16[384,128]{1,0:T(8,128)(2,1)} %x_hbm.1, bf16[48,3696]{1,0:T(8,128)(2,1)} %gate_hbm.1, bf16[48,3696]{1,0:T(8,128)(2,1)} %up_hbm.1, bf16[48,3696]{1,0:T(8,128)(2,1)} %grad_hbm.1, bf16[3696,128]{1,0:T(8,128)(2,1)} %bitcast.2, bf16[3696,128]{1,0:T(8,128)(2,1)} %bitcast.3), custom_call_target="tpu_custom_call" | custom-call | tf_op jit(solution)/shard_map/pallas_call | solution.py:371
  93.3 2.3 %shard_map.86 = (bf16[384,128]{1,0:T(8,128)(2,1)}, bf16[64,3696]{1,0:T(8,128)(2,1)}, bf16[64,3696]{1,0:T(8,128)(2,1)}) custom-call(bf16[384,128]{1,0:T(8,128)(2,1)} %get-tuple-element.5.ig_in, bf16[4,64,1920]{2,1,0:T(8,128)(2,1)} %get-tuple-element.6.w_out), custom_call_target="tpu_custom_call" | custom-call | tf_op jit(solution)/shard_map/pallas_call | solution.py:384

commit v4 on v3

--- a/solution.py
+++ b/solution.py
@@ -166,24 +166,27 @@
         moved[way].append((send(g[k].at[rows], g[k].at[rows], to),))
 
     swap(0)
+    loads[3].wait()
+    xt_own[...] = x_ref[...].astype(F32).T.astype(BF)
+    xt_rows = pl.ds(pl.multiple_of(x * WIDE, WIDE), WIDE)
+    xt_cols = pl.ds(pl.multiple_of(y * TB, 128), TB)
+    xt_x = [send(xt_own, xt.at[xt_rows, xt_cols], at(x_=turn(x, o, NX))) for o in (1, 2, 3)]
+    xt_local = local(xt_own, xt.at[xt_rows, xt_cols])
     gated(1)
     swap(1)
     swapped[0][0][1].wait_recv()
     for way in (1, -1):
         pass_on(0, way)
     gated(2)
-    swap(2)
     for m in (2, 3):
         swapped[0][0][m].wait_recv()
     swapped[0][1].wait()
     for way in (1, -1):
         pass_on(1, way)
-    loads[3].wait()
-    xt_own[...] = x_ref[...].astype(F32).T.astype(BF)
-    xt_rows = pl.ds(pl.multiple_of(x * WIDE, WIDE), WIDE)
-    xt_cols = pl.ds(pl.multiple_of(y * TB, 128), TB)
-    xt_x = [send(xt_own, xt.at[xt_rows, xt_cols], at(x_=turn(x, o, NX))) for o in (1, 2, 3)]
-    xt_local = local(xt_own, xt.at[xt_rows, xt_cols])
+    for copy in xt_x:
+        copy.wait_recv()
+    xt_local.wait()
+    xt_y = [send(xt.at[:, xt_cols], xt.at[:, xt_cols], at(y_=turn(y, o, NY))) for o in (1, 2, 3)]
     for load in w_loads:
         load.wait()
 
@@ -196,10 +199,7 @@
         for o in (1, 2, 3)
     ]
     w_local = local(own_w.at[x, w_half], w_all.at[w_half, w_cols])
-    for copy in xt_x:
-        copy.wait_recv()
-    xt_local.wait()
-    xt_y = [send(xt.at[:, xt_cols], xt.at[:, xt_cols], at(y_=turn(y, o, NY))) for o in (1, 2, 3)]
+    swap(2)
 
     def weight_piece(k, lo):
         n = min(256, CHUNKS[k] - lo)
@@ -285,7 +285,7 @@
                 for copy in moved[way][k * events + e]:
                     copy.wait_recv()
                 pass_on(k * events + e + 2, way)
-            if (k, e) == (1, 0):
+            if (k, e) == (1, 2):
                 for copy in xt_y:
                     copy.wait_recv()
             if (k, e) == (1, 4):
@@ -298,11 +298,12 @@
             for b in parts_at.get((k, e), ()):
                 input_part(b)
             if k >= 1:
-                if e < 3 and e * 256 < CHUNKS[k - 1]:
-                    weight_piece(k - 1, e * 256)
-                if e == 2:
+                piece = e - (2 if k == 1 else 0)
+                if 0 <= piece < 3 and piece * 256 < CHUNKS[k - 1]:
+                    weight_piece(k - 1, piece * 256)
+                if piece == 2:
                     exchange(k - 1)
-                if e == 4:
+                if piece == (4 if k == 1 else 3):
                     give_back(k - 1)
             for b in sums_at.get((k, e), ()):
                 input_sum(b)

time: 97.1 us -> 90.9 us (0.936); the launches traced: 95.6 us -> 90.4 us
  Pallas kernels: 94.9 us -> 89.7 us
    pallas_call x1, Pallas kernels: 92.7 us -> 87.5 us  [on_device(): pl.pallas_call(kernel, out_shape=(jax.ShapeDtypeStruct((TB, WIDE), BF), j...]
where the time goes in v4:
time: 90.9 us; the launch traced here: 90.4 us
  Pallas kernels  89.7 us (99%)
    pallas_call x1, Pallas kernels, on_device(): pl.pallas_call(kernel, out_shape=(jax.ShapeDtypeStruct((TB, WIDE), BF), j...  87.5 us
    pallas_call x1, Pallas kernels, on_device(): pl.pallas_call(unpack, out_shape=(jax.ShapeDtypeStruct((TB, WIDE), BF), j...  2.26 us

profile of v4, /device:TPU:16, one launch (start us, length us, event | category | flops | bytes accessed | tf_op | source)
XLA Modules:
  0.0 90.4 jit_solution(9486184792158788186)
XLA Ops:
  0.6 87.5 %shard_map.85 = (bf16[384,128]{1,0:T(8,128)(2,1)}, bf16[4,64,1920]{2,1,0:T(8,128)(2,1)}) custom-call(bf16[384,128]{1,0:T(8,128)(2,1)} %x_hbm.1, bf16[48,3696]{1,0:T(8,128)(2,1)} %gate_hbm.1, bf16[48,3696]{1,0:T(8,128)(2,1)} %up_hbm.1, bf16[48,3696]{1,0:T(8,128)(2,1)} %grad_hbm.1, bf16[3696,128]{1,0:T(8,128)(2,1)} %bitcast.2, bf16[3696,128]{1,0:T(8,128)(2,1)} %bitcast.3), custom_call_target="tpu_custom_call" | custom-call | tf_op jit(solution)/shard_map/pallas_call | solution.py:372
  88.1 2.3 %shard_map.86 = (bf16[384,128]{1,0:T(8,128)(2,1)}, bf16[64,3696]{1,0:T(8,128)(2,1)}, bf16[64,3696]{1,0:T(8,128)(2,1)}) custom-call(bf16[384,128]{1,0:T(8,128)(2,1)} %get-tuple-element.5.ig_in, bf16[4,64,1920]{2,1,0:T(8,128)(2,1)} %get-tuple-element.6.w_out), custom_call_target="tpu_custom_call" | custom-call | tf_op jit(solution)/shard_map/pallas_call | solution.py:385

commit v5 on v4

--- a/solution.py
+++ b/solution.py
@@ -276,7 +276,7 @@
 
     over_core = []
     parts_at = {(1, 6): (0,), (2, 1): (-1, 1), (2, 3): (-2, 2), (2, 5): (-3, 3), (2, 6): (4,)}
-    sums_at = {(2, 1): (0,), (2, 4): (-1, 1), (2, 6): (-2, 2)}
+    sums_at = {(2, 1): (0,), (2, 4): (-1, 1)}
     for k in range(len(CHUNKS)):
         for e in range(events):
             if e == 4 and k < last:
@@ -311,9 +311,11 @@
     for lo in range(0, CHUNKS[last], 256):
         weight_piece(last, lo)
     exchange(last)
+    for b in (-2, 2):
+        input_sum(b)
+    give_back(last)
     for b in (-3, 3, 4):
         input_sum(b)
-    give_back(last)
 
     for o in (1, 2, 3):
         for parity in (0, 1):

time: 90.9 us -> 89.3 us (0.982)
  Pallas kernels: 89.7 us -> 88.5 us
    pallas_call x1, Pallas kernels: 87.5 us -> 86.3 us  [on_device(): pl.pallas_call(kernel, out_shape=(jax.ShapeDtypeStruct((TB, WIDE), BF), j...]
where the time goes in v5:
time: 89.3 us; the launch traced here: 89.2 us
  Pallas kernels  88.5 us (99%)
    pallas_call x1, Pallas kernels, on_device(): pl.pallas_call(kernel, out_shape=(jax.ShapeDtypeStruct((TB, WIDE), BF), j...  86.3 us
    pallas_call x1, Pallas kernels, on_device(): pl.pallas_call(unpack, out_shape=(jax.ShapeDtypeStruct((TB, WIDE), BF), j...  2.26 us

profile of v5, /device:TPU:16, one launch (start us, length us, event | category | flops | bytes accessed | tf_op | source)
XLA Modules:
  0.0 89.2 jit_solution(6202937904909753167)
XLA Ops:
  0.6 86.3 %shard_map.85 = (bf16[384,128]{1,0:T(8,128)(2,1)}, bf16[4,64,1920]{2,1,0:T(8,128)(2,1)}) custom-call(bf16[384,128]{1,0:T(8,128)(2,1)} %x_hbm.1, bf16[48,3696]{1,0:T(8,128)(2,1)} %gate_hbm.1, bf16[48,3696]{1,0:T(8,128)(2,1)} %up_hbm.1, bf16[48,3696]{1,0:T(8,128)(2,1)} %grad_hbm.1, bf16[3696,128]{1,0:T(8,128)(2,1)} %bitcast.2, bf16[3696,128]{1,0:T(8,128)(2,1)} %bitcast.3), custom_call_target="tpu_custom_call" | custom-call | tf_op jit(solution)/shard_map/pallas_call | solution.py:374
  86.9 2.3 %shard_map.86 = (bf16[384,128]{1,0:T(8,128)(2,1)}, bf16[64,3696]{1,0:T(8,128)(2,1)}, bf16[64,3696]{1,0:T(8,128)(2,1)}) custom-call(bf16[384,128]{1,0:T(8,128)(2,1)} %get-tuple-element.5.ig_in, bf16[4,64,1920]{2,1,0:T(8,128)(2,1)} %get-tuple-element.6.w_out), custom_call_target="tpu_custom_call" | custom-call | tf_op jit(solution)/shard_map/pallas_call | solution.py:387

commit v6 on v5

--- a/solution.py
+++ b/solution.py
@@ -68,6 +68,10 @@
         locals_.append(copy)
         return copy
 
+    loads = [
+        local(src, dst)
+        for src, dst in ((gate_hbm, gate_ref), (up_hbm, up_ref), (grad_hbm, grad_ref), (x_hbm, x_ref))
+    ]
     partners = [at(x_=turn(x, o, NX)) for o in (1, 2, 3)]
     partners += [at(y_=turn(y, o, NY)) for o in (1, 2, 3)]
     partners += [at(z_=turn(z, o, NZ)) for o in (1, -1)]
@@ -76,19 +80,6 @@
     for device in partners:
         pl.semaphore_signal(barrier, inc=1, device_id=device, device_id_type=pl.DeviceIdType.MESH)
 
-    loads = [
-        local(src, dst)
-        for src, dst in ((gate_hbm, gate_ref), (up_hbm, up_ref), (grad_hbm, grad_ref), (x_hbm, x_ref))
-    ]
-    w_loads = [
-        local(
-            (gw_hbm, uw_hbm)[which].at[pl.ds(first, columns)],
-            own_w.at[block, pl.ds(there, columns)],
-        )
-        for which, first, block, there, columns in PIECES
-    ]
-    for block, first, end in ROW_PADS:
-        own_w[block, first:end, :] = jnp.zeros((end - first, WIDE), BF)
     for block, first, end in PADS:
         own_g[block, :, first:end] = jnp.zeros((ROWS, end - first), BF)
     for load in loads[:3]:
@@ -166,6 +157,15 @@
         moved[way].append((send(g[k].at[rows], g[k].at[rows], to),))
 
     swap(0)
+    w_loads = [
+        local(
+            (gw_hbm, uw_hbm)[which].at[pl.ds(first, columns)],
+            own_w.at[block, pl.ds(there, columns)],
+        )
+        for which, first, block, there, columns in PIECES
+    ]
+    for block, first, end in ROW_PADS:
+        own_w[block, first:end, :] = jnp.zeros((end - first, WIDE), BF)
     loads[3].wait()
     xt_own[...] = x_ref[...].astype(F32).T.astype(BF)
     xt_rows = pl.ds(pl.multiple_of(x * WIDE, WIDE), WIDE)
@@ -391,8 +391,16 @@
             jax.ShapeDtypeStruct((HALF, UNITS), BF),
             jax.ShapeDtypeStruct((HALF, UNITS), BF),
         ),
-        in_specs=[in_vmem] * 2,
-        out_specs=(in_vmem,) * 3,
+        grid=(2,),
+        in_specs=[
+            pl.BlockSpec((TB // 2, WIDE), lambda i: (i, 0)),
+            pl.BlockSpec((NX, HALF // 2, XB), lambda i: (0, i, 0)),
+        ],
+        out_specs=(
+            pl.BlockSpec((TB // 2, WIDE), lambda i: (i, 0)),
+            pl.BlockSpec((HALF // 2, UNITS), lambda i: (i, 0)),
+            pl.BlockSpec((HALF // 2, UNITS), lambda i: (i, 0)),
+        ),
     )(input_grad, packed)
 
 

time: 89.3 us -> 89.1 us (level)
  no operation moved by 1% of the time
where the time goes in v6:
time: 89.1 us; the launch traced here: 89 us
  Pallas kernels  88.4 us (99%)
    pallas_call x1, Pallas kernels, on_device(): pl.pallas_call(kernel, out_shape=(jax.ShapeDtypeStruct((TB, WIDE), BF), j...  86.3 us
    pallas_call x1, Pallas kernels, on_device(): pl.pallas_call(unpack, out_shape=(jax.ShapeDtypeStruct((TB, WIDE), BF), j...  2.07 us

profile of v6, /device:TPU:16, one launch (start us, length us, event | category | flops | bytes accessed | tf_op | source)
XLA Modules:
  0.0 89.0 jit_solution(6955428477644868983)
XLA Ops:
  0.6 86.3 %shard_map.85 = (bf16[384,128]{1,0:T(8,128)(2,1)}, bf16[4,64,1920]{2,1,0:T(8,128)(2,1)}) custom-call(bf16[384,128]{1,0:T(8,128)(2,1)} %x_hbm.1, bf16[48,3696]{1,0:T(8,128)(2,1)} %gate_hbm.1, bf16[48,3696]{1,0:T(8,128)(2,1)} %up_hbm.1, bf16[48,3696]{1,0:T(8,128)(2,1)} %grad_hbm.1, bf16[3696,128]{1,0:T(8,128)(2,1)} %bitcast.2, bf16[3696,128]{1,0:T(8,128)(2,1)} %bitcast.3), custom_call_target="tpu_custom_call" | custom-call | tf_op jit(solution)/shard_map/pallas_call | solution.py:374
  86.9 2.1 %shard_map.86 = (bf16[384,128]{1,0:T(8,128)(2,1)}, bf16[64,3696]{1,0:T(8,128)(2,1)}, bf16[64,3696]{1,0:T(8,128)(2,1)}) custom-call(bf16[384,128]{1,0:T(8,128)(2,1)} %get-tuple-element.5.ig_in, bf16[4,64,1920]{2,1,0:T(8,128)(2,1)} %get-tuple-element.6.w_out), custom_call_target="tpu_custom_call" | custom-call | tf_op jit(solution)/shard_map/pallas_call | solution.py:387

commit v7 on v6

--- a/solution.py
+++ b/solution.py
@@ -16,8 +16,8 @@
 DB = NX * WIDE
 TB = 2 * ZB
 HALF = WIDE // 2
-CHUNKS = (640, 640, 640)
-STARTS = (0, 640, 1280)
+CHUNKS = (640, 512, 768)
+STARTS = (0, 640, 1152)
 N_COPIES = 112
 BF, F32 = jnp.bfloat16, jnp.float32
 
@@ -89,7 +89,8 @@
 
     def gated(k):
         for t in range(TILES):
-            chunks = [(tile % (XB // WIDE)) * WIDE // CHUNKS[0] for tile in (t, TILES + t)]
+            places = [tile % (XB // WIDE) * WIDE for tile in (t, TILES + t)]
+            chunks = [sum(start <= place for start in STARTS) - 1 for place in places]
             if k not in chunks or t in done:
                 continue
             done.add(t)

time: 89.1 us -> 88.3 us (level)
  the two profiles are of different devices: /device:TPU:16 before, /device:TPU:1 now
where the time goes in v7:
time: 88.3 us; the launch traced here: 88.2 us
  Pallas kernels  87.5 us (99%)
    pallas_call x1, Pallas kernels, on_device(): pl.pallas_call(kernel, out_shape=(jax.ShapeDtypeStruct((TB, WIDE), BF), j...  85.5 us
    pallas_call x1, Pallas kernels, on_device(): pl.pallas_call(unpack, out_shape=(jax.ShapeDtypeStruct((TB, WIDE), BF), j...  2.07 us

profile of v7, /device:TPU:1, one launch (start us, length us, event | category | flops | bytes accessed | tf_op | source)
XLA Modules:
  0.0 88.2 jit_solution(799391316194473687)
XLA Ops:
  0.6 85.5 %shard_map.85 = (bf16[384,128]{1,0:T(8,128)(2,1)}, bf16[4,64,1920]{2,1,0:T(8,128)(2,1)}) custom-call(bf16[384,128]{1,0:T(8,128)(2,1)} %x_hbm.1, bf16[48,3696]{1,0:T(8,128)(2,1)} %gate_hbm.1, bf16[48,3696]{1,0:T(8,128)(2,1)} %up_hbm.1, bf16[48,3696]{1,0:T(8,128)(2,1)} %grad_hbm.1, bf16[3696,128]{1,0:T(8,128)(2,1)} %bitcast.2, bf16[3696,128]{1,0:T(8,128)(2,1)} %bitcast.3), custom_call_target="tpu_custom_call" | custom-call | tf_op jit(solution)/shard_map/pallas_call | solution.py:375
  86.1 2.1 %shard_map.86 = (bf16[384,128]{1,0:T(8,128)(2,1)}, bf16[64,3696]{1,0:T(8,128)(2,1)}, bf16[64,3696]{1,0:T(8,128)(2,1)}) custom-call(bf16[384,128]{1,0:T(8,128)(2,1)} %get-tuple-element.5.ig_in, bf16[4,64,1920]{2,1,0:T(8,128)(2,1)} %get-tuple-element.6.w_out), custom_call_target="tpu_custom_call" | custom-call | tf_op jit(solution)/shard_map/pallas_call | solution.py:388

commit v8 on v7

--- a/solution.py
+++ b/solution.py
@@ -302,9 +302,9 @@
                 piece = e - (2 if k == 1 else 0)
                 if 0 <= piece < 3 and piece * 256 < CHUNKS[k - 1]:
                     weight_piece(k - 1, piece * 256)
-                if piece == 2:
+                if piece == (2 if k == 1 else 1):
                     exchange(k - 1)
-                if piece == (4 if k == 1 else 3):
+                if piece == (4 if k == 1 else 2):
                     give_back(k - 1)
             for b in sums_at.get((k, e), ()):
                 input_sum(b)

time: 88.3 us -> 88.5 us (level)
  no operation moved by 1% of the time
where the time goes in v8:
time: 88.5 us; the launch traced here: 88.3 us
  Pallas kernels  87.7 us (99%)
    pallas_call x1, Pallas kernels, on_device(): pl.pallas_call(kernel, out_shape=(jax.ShapeDtypeStruct((TB, WIDE), BF), j...  85.6 us
    pallas_call x1, Pallas kernels, on_device(): pl.pallas_call(unpack, out_shape=(jax.ShapeDtypeStruct((TB, WIDE), BF), j...  2.07 us

profile of v8, /device:TPU:1, one launch (start us, length us, event | category | flops | bytes accessed | tf_op | source)
XLA Modules:
  0.0 88.3 jit_solution(11496105449844947446)
XLA Ops:
  0.6 85.6 %shard_map.85 = (bf16[384,128]{1,0:T(8,128)(2,1)}, bf16[4,64,1920]{2,1,0:T(8,128)(2,1)}) custom-call(bf16[384,128]{1,0:T(8,128)(2,1)} %x_hbm.1, bf16[48,3696]{1,0:T(8,128)(2,1)} %gate_hbm.1, bf16[48,3696]{1,0:T(8,128)(2,1)} %up_hbm.1, bf16[48,3696]{1,0:T(8,128)(2,1)} %grad_hbm.1, bf16[3696,128]{1,0:T(8,128)(2,1)} %bitcast.2, bf16[3696,128]{1,0:T(8,128)(2,1)} %bitcast.3), custom_call_target="tpu_custom_call" | custom-call | tf_op jit(solution)/shard_map/pallas_call | solution.py:375
  86.3 2.1 %shard_map.86 = (bf16[384,128]{1,0:T(8,128)(2,1)}, bf16[64,3696]{1,0:T(8,128)(2,1)}, bf16[64,3696]{1,0:T(8,128)(2,1)}) custom-call(bf16[384,128]{1,0:T(8,128)(2,1)} %get-tuple-element.5.ig_in, bf16[4,64,1920]{2,1,0:T(8,128)(2,1)} %get-tuple-element.6.w_out), custom_call_target="tpu_custom_call" | custom-call | tf_op jit(solution)/shard_map/pallas_call | solution.py:388
